TPU v7x, 128 devices: a whole 4x4x4 slice. The times are simulated.
128 devices in a mesh: tm: 4 (over y), lat: 4 (over x_lo, core), lon: 8 (over z, x_hi).
Axes of the slice: x: 4 (x_hi: 2, x_lo: 2; x = x_hi * 2 + x_lo), y: 4, z: 4, core: 2. Of those that a mesh axis runs over, the one named last changes fastest.
Arguments:
- latents: bfloat16 [4, 64, 128, 1536], P('tm', 'lat', 'lon'), may hold values from -450 to 450
- ada_shift: float32 [1536], replicated, may hold values from -3 to 3
- ada_scale: float32 [1536], replicated, may hold values from -0.5 to 0.5
- ada_gate: float32 [1536], replicated, may hold values from 0.5 to 1.5
- w_query: bfloat16 [1536, 1536], replicated, may hold values from -2 to 2
- w_key: bfloat16 [1536, 1536], replicated, may hold values from -2 to 2
- w_value: bfloat16 [1536, 1536], replicated, may hold values from -0.15625 to 0.15625
- w_out: bfloat16 [1536, 1536], replicated, may hold values from -0.15625 to 0.15625
- query_gain: float32 [1536], replicated, may hold values from 0.3 to 6.5
- key_gain: float32 [1536], replicated, may hold values from 0.3 to 6.5
Outputs:
- branch_out: bfloat16 [4, 64, 128, 1536], P('tm', 'lat', 'lon')
All inputs are finite; a program needn't handle non-finite values.
Results may differ from a plain program's by a relative error of at most 0.0075.
Values may be sent and summed in bfloat16 or wider, within the bound.
A program may use at most 128 MiB of HBM per device.

v0:
```python
import jax
import jax.numpy as jnp
from jax import lax
from jax.sharding import PartitionSpec as P

HEADS = 12
HEAD_DIM = 128


def padded(cells, sides, width, closed):
    for axis, dim in sides:
        count = lax.axis_size(axis)
        ends = count if closed else count - 1
        head = lax.slice_in_dim(cells, 0, width, axis=dim)
        tail = lax.slice_in_dim(cells, cells.shape[dim] - width, cells.shape[dim], axis=dim)
        cells = jnp.concatenate(
            [
                lax.ppermute(tail, axis, [(i, (i + 1) % count) for i in range(ends)]),
                cells,
                lax.ppermute(head, axis, [((i + 1) % count, i) for i in range(ends)]),
            ],
            axis=dim,
        )
    return cells


def modulate(latents, ada_shift, ada_scale):
    values_f = latents.astype(jnp.float32)
    mean_value = jnp.mean(values_f, axis=-1, keepdims=True)
    centred = values_f - mean_value
    variance = jnp.mean(centred * centred, axis=-1, keepdims=True)
    return (centred * lax.rsqrt(variance + 1e-06) * (1.0 + ada_scale) + ada_shift).astype(
        jnp.bfloat16
    )


def rms_gain(projected, gain_vector):
    mean_square = jnp.mean(projected * projected, axis=-1, keepdims=True)
    return (projected * lax.rsqrt(mean_square + 1e-06) * gain_vector).astype(jnp.bfloat16)


def frame_halo(block):
    return padded(block, (("tm", 0),), 1, False)


def widen_cells(block):
    return padded(block, (("lat", 1), ("lon", 2)), 3, True)


def extend(block):
    return widen_cells(frame_halo(block))


def shards(
    latents, ada_shift, ada_scale, ada_gate, w_query, w_key, w_value, w_out, query_gain, key_gain
):
    frame_count, lat_count, lon_count, model_width = latents.shape
    normed = modulate(latents, ada_shift, ada_scale)
    token_rows = normed.reshape(-1, model_width)
    query_rows = rms_gain(
        jnp.dot(token_rows, w_query, preferred_element_type=jnp.float32), query_gain
    )
    query_grid = query_rows.reshape(frame_count, lat_count, lon_count, HEADS, HEAD_DIM)
    key_rows = rms_gain(jnp.dot(token_rows, w_key, preferred_element_type=jnp.float32), key_gain)
    value_rows = jnp.dot(token_rows, w_value, preferred_element_type=jnp.float32).astype(
        jnp.bfloat16
    )
    joined = jnp.concatenate([key_rows, value_rows], axis=-1).reshape(
        frame_count, lat_count, lon_count, 2 * model_width
    )
    widened = extend(joined)
    head_shape = widened.shape[:3] + (HEADS, HEAD_DIM)
    key_grid = widened[..., :model_width].reshape(head_shape)
    value_grid = widened[..., model_width:].reshape(head_shape)
    band = 8
    band_count = lat_count // band
    key_rows_n = band + 6
    key_cols_n = lon_count + 6
    query_count = band * lon_count
    time_first = lax.axis_index("tm") * frame_count
    lat_first = lax.axis_index("lat") * lat_count
    all_frames = frame_count * lax.axis_size("tm")
    all_lats = lat_count * lax.axis_size("lat")
    query_index = jnp.arange(query_count, dtype=jnp.int32)
    query_lat = (query_index // lon_count)[:, None, None]
    query_lon = (query_index % lon_count)[:, None, None]
    key_lat = jnp.arange(key_rows_n, dtype=jnp.int32)[None, :, None]
    key_lon = jnp.arange(key_cols_n, dtype=jnp.int32)[None, None, :]
    in_window = (
        (key_lat - query_lat >= 0)
        & (key_lat - query_lat <= 6)
        & (key_lon - query_lon >= 0)
        & (key_lon - query_lon <= 6)
    )
    frame_steps = jnp.arange(3, dtype=jnp.int32)
    lat_steps = jnp.arange(key_rows_n, dtype=jnp.int32)
    results = []
    key_time = time_first + 0 + frame_steps - 1
    time_inside = (key_time >= 0) & (key_time < all_frames)
    for band_idx in range(band_count):
        row_start = band_idx * band
        global_lat = lat_first + row_start + lat_steps - 3
        lat_inside = (global_lat >= 0) & (global_lat < all_lats)
        allowed = (
            in_window[:, None, :, :]
            & time_inside[None, :, None, None]
            & lat_inside[None, None, :, None]
        )
        allowed = allowed.reshape(query_count, -1)
        query_block = query_grid[0, row_start : row_start + band].reshape(
            query_count, HEADS, HEAD_DIM
        )
        key_block = key_grid[0:3, row_start : row_start + key_rows_n]
        value_block = value_grid[0:3, row_start : row_start + key_rows_n]
        scores = jnp.einsum(
            "qhd,tljhd->hqtlj", query_block, key_block, preferred_element_type=jnp.float32
        )
        scores = scores.reshape(HEADS, query_count, -1) * HEAD_DIM ** (-0.5)
        scores = jnp.where(allowed[None], scores, -1e30)
        row_max = jnp.max(scores, axis=-1, keepdims=True)
        raw_weights = jnp.exp(scores - row_max)
        probs = (raw_weights / jnp.sum(raw_weights, axis=-1, keepdims=True)).astype(jnp.bfloat16)
        probs = probs.reshape(HEADS, query_count, 3, key_rows_n, key_cols_n)
        attended = jnp.einsum(
            "hqtlj,tljhd->qhd", probs, value_block, preferred_element_type=jnp.float32
        )
        results.append(attended.astype(jnp.bfloat16).reshape(query_count, model_width))
    attended_rows = jnp.concatenate(results, axis=0)
    projected = jnp.dot(attended_rows, w_out, preferred_element_type=jnp.float32) * ada_gate
    return projected.astype(jnp.bfloat16).reshape(latents.shape)


def solution(mesh):
    return jax.shard_map(
        shards,
        mesh=mesh,
        in_specs=(P("tm", "lat", "lon", None), P(), P(), P(), P(), P(), P(), P(), P(), P()),
        out_specs=P("tm", "lat", "lon", None),
        check_vma=False,
    )
```

profile of v0, /device:TPU:16, one launch (start us, length us, event | category | flops | bytes accessed | tf_op | source)
XLA Modules:
  0.0 209.6 jit_solution(9702452180141395227)
XLA Ops:
  0.0 1.3 convert_reduce_fusion
  1.3 1.5 fusion.17
  2.8 0.7 broadcast_add_fusion
  3.5 1.6 fusion.20
  5.2 0.0 slice-start.1
  5.2 0.0 slice-start.2
  5.2 4.0 %multiply_reduce_fusion.1 = (f32[256]{0:T(256)S(1)}, f32[256,1536]{1,0:T(8,128)S(1)}) fusion(bf16[256,1536]{1,0:T(8,128)(2,1)S(1)} %bitcast.45, bf16[1536,1536]{1,0:T(8,128)(2,1)} %param.15), kind=kOutput, calls=%fused_computation.41 | convolution fusion | flops 1208745728 | bytes 7078912 | tf_op jit(solution)/shard_map/dot_general | solution.py:64
  9.2 0.0 slice-done
  9.2 0.0 slice-done.1
  9.2 0.0 copy-start.6
  9.2 0.0 slice-start.3
  9.2 1.4 convolution_convert_fusion
  10.6 0.0 copy-done.6
  10.6 0.2 multiply_convert_fusion.1
  10.8 0.2 pad_maximum_fusion.6
  11.0 3.2 %collective-permute-start = (bf16[1,16,16,3072]{3,2,1,0:T(8,128)(2,1)S(1)}, bf16[1,16,16,3072]{3,2,1,0:T(8,128)(2,1)S(1)}, u32[]{:S(2)}, u32[]{:S(2)}) collective-permute-start(bf16[1,16,16,3072]{3,2,1,0:T(8,128)(2,1)S(1)} %bitcast.40), channel_id=1, source_target_pairs={{0,32},{32,64},{64,96},{1,33},{33,65},{65,97},{2,34},{34,66},{66,9... | collective-permute-start | bytes 4718600 | tf_op jit(solution)/shard_map/ppermute | solution.py:18
  14.2 2.7 %collective-permute-start.1 = (bf16[1,16,16,3072]{3,2,1,0:T(8,128)(2,1)S(1)}, bf16[1,16,16,3072]{3,2,1,0:T(8,128)(2,1)S(1)}, u32[]{:S(2)}, u32[]{:S(2)}) collective-permute-start(bf16[1,16,16,3072]{3,2,1,0:T(8,128)(2,1)S(1)} %bitcast.41), channel_id=1, source_target_pairs={{32,0},{64,32},{96,64},{33,1},{65,33},{97,65},{34,2},{66,34},{98,6... | collective-permute-start | bytes 4718600 | tf_op jit(solution)/shard_map/ppermute | solution.py:20
  16.9 1.5 multiply_reduce_fusion
  18.4 0.0 copy-start.7
  18.4 30.7 %collective-permute-done = bf16[1,16,16,3072]{3,2,1,0:T(8,128)(2,1)S(1)} collective-permute-done((bf16[1,16,16,3072]{3,2,1,0:T(8,128)(2,1)S(1)}, bf16[1,16,16,3072]{3,2,1,0:T(8,128)(2,1)S(1)}, u32[]{:S(2)}, u32[]{:S(2)}) %collective-permute-start) | collective-permute-done | bytes 1572896 | tf_op jit(solution)/shard_map/ppermute | solution.py:18
  49.0 2.9 %collective-permute-done.1 = bf16[1,16,16,3072]{3,2,1,0:T(8,128)(2,1)S(1)} collective-permute-done((bf16[1,16,16,3072]{3,2,1,0:T(8,128)(2,1)S(1)}, bf16[1,16,16,3072]{3,2,1,0:T(8,128)(2,1)S(1)}, u32[]{:S(2)}, u32[]{:S(2)}) %collective-permute-start.1) | collective-permute-done | bytes 1572896 | tf_op jit(solution)/shard_map/ppermute | solution.py:20
  52.0 1.5 pad_maximum_fusion.9
  53.5 0.2 copy-done
  53.7 0.0 collective-permute-start.2
  53.7 1.7 collective-permute-start.3
  55.4 1.1 multiply_convert_fusion
  56.5 2.4 %reshape.266 = bf16[1,16,16,12,128]{4,3,2,1,0:T(8,128)(2,1)} reshape(bf16[256,1536]{1,0:T(8,128)(2,1)} %multiply_convert_fusion) | data formatting | bytes 1572864 | tf_op jit(solution)/shard_map/reshape | solution.py:63
  58.9 2.2 %fusion.53 = (bf16[1,8,16,12,128]{4,3,2,1,0:T(8,128)(2,1)S(1)}, bf16[1,8,16,12,128]{4,3,2,1,0:T(8,128)(2,1)}) fusion(bf16[1,16,16,12,128]{4,3,2,1,0:T(8,128)(2,1)} %reshape.266), kind=kLoop, calls=%fused_computation.79 | loop fusion | bytes 1572864 | tf_op jit(solution)/shard_map/slice | solution.py:110
  61.1 0.8 copy.41
  62.0 1.9 copy.45
  63.9 10.2 %collective-permute-done.2 = bf16[3,3,16,3072]{3,2,1,0:T(8,128)(2,1)} collective-permute-done((bf16[3,3,16,3072]{3,2,1,0:T(8,128)(2,1)}, bf16[3,3,16,3072]{3,2,1,0:T(8,128)(2,1)}, u32[]{:S(2)}, u32[]{:S(2)}) %collective-permute-start.2) | collective-permute-done | bytes 884768 | tf_op jit(solution)/shard_map/ppermute | solution.py:18
  74.1 0.9 collective-permute-done.3
  75.0 3.8 %pad_maximum_fusion.5 = (bf16[3,22,3,3072]{3,2,1,0:T(4,128)(2,1)S(1)}, bf16[3,22,3,3072]{3,2,1,0:T(4,128)(2,1)S(1)}) fusion(bf16[3,3,16,3072]{3,2,1,0:T(8,128)(2,1)} %collective-permute-done.3, bf16[3,3,16,3072]{3,2,1,0:T(8,128)(2,1)} %collective-permute-done.2, bf16[1,16,16,3072]{3,2,1,0:T(8,128)(2,1)} %copy-done, ...), kind=kLoop, calls=%fused_computation.32 | loop fusion | flops 12165120 | bytes 8921088 | tf_op jit(solution)/shard_map/slice | solution.py:15
  78.8 0.5 copy.36
  79.3 2.8 %collective-permute-start.4 = (bf16[3,22,3,3072]{3,1,2,0:T(8,128)(2,1)S(1)}, bf16[3,22,3,3072]{3,1,2,0:T(8,128)(2,1)S(1)}, u32[]{:S(2)}, u32[]{:S(2)}) collective-permute-start(bf16[3,22,3,3072]{3,1,2,0:T(8,128)(2,1)S(1)} %copy.36), channel_id=1, source_target_pairs={{0,1},{1,2},{2,3},{3,4},{4,5},{5,6},{6,7},{7,0},{8,9},{9,10},{10,1... | collective-permute-start | bytes 3649544 | tf_op jit(solution)/shard_map/ppermute | solution.py:18
  82.1 0.5 copy.37
  82.5 0.0 copy-start.1
  82.5 3.7 %collective-permute-start.5 = (bf16[3,22,3,3072]{3,1,2,0:T(8,128)(2,1)S(1)}, bf16[3,22,3,3072]{3,1,2,0:T(8,128)(2,1)S(1)}, u32[]{:S(2)}, u32[]{:S(2)}) collective-permute-start(bf16[3,22,3,3072]{3,1,2,0:T(8,128)(2,1)S(1)} %copy.37), channel_id=1, source_target_pairs={{1,0},{2,1},{3,2},{4,3},{5,4},{6,5},{7,6},{0,7},{9,8},{10,9},{11,1... | collective-permute-start | bytes 3649544 | tf_op jit(solution)/shard_map/ppermute | solution.py:20
  86.4 0.2 and_and_fusion.1
  86.6 28.6 %collective-permute-done.4 = bf16[3,22,3,3072]{3,1,2,0:T(8,128)(2,1)S(1)} collective-permute-done((bf16[3,22,3,3072]{3,1,2,0:T(8,128)(2,1)S(1)}, bf16[3,22,3,3072]{3,1,2,0:T(8,128)(2,1)S(1)}, u32[]{:S(2)}, u32[]{:S(2)}) %collective-permute-start.4) | collective-permute-done | bytes 1216544 | tf_op jit(solution)/shard_map/ppermute | solution.py:18
  115.2 1.0 copy.38
  116.2 26.2 %collective-permute-done.5 = bf16[3,22,3,3072]{3,1,2,0:T(8,128)(2,1)S(1)} collective-permute-done((bf16[3,22,3,3072]{3,1,2,0:T(8,128)(2,1)S(1)}, bf16[3,22,3,3072]{3,1,2,0:T(8,128)(2,1)S(1)}, u32[]{:S(2)}, u32[]{:S(2)}) %collective-permute-start.5) | collective-permute-done | bytes 1216544 | tf_op jit(solution)/shard_map/ppermute | solution.py:20
  142.5 1.0 copy.39
  143.5 11.0 %pad_maximum_fusion = bf16[3,22,22,3072]{3,2,1,0:T(8,128)(2,1)} fusion(bf16[3,22,3,3072]{3,2,1,0:T(4,128)(2,1)S(1)} %copy.39, bf16[3,3,16,3072]{3,2,1,0:T(8,128)(2,1)} %collective-permute-done.3, bf16[1,16,16,3072]{3,2,1,0:T(8,128)(2,1)S(1)} %copy-done.1, bf16[1,16,16,3072]{3,2,1,0:T(8,128)(2,1)S(1)} %bitcast.44, ...), kind=kLoop, calls=%fused_computation | loop fusion | flops 62447616 | bytes 17842176 | tf_op jit(solution)/shard_map/concatenate | solution.py:16
  154.5 8.4 %fusion.50 = (bf16[3,22,22,1536]{3,2,1,0:T(8,128)(2,1)}, bf16[3,22,22,1536]{3,2,1,0:T(8,128)(2,1)}) fusion(bf16[3,22,22,3072]{3,2,1,0:T(8,128)(2,1)} %pad_maximum_fusion), kind=kLoop, calls=%fused_computation.76 | loop fusion | bytes 17842176 | tf_op jit(solution)/shard_map/slice | solution.py:74
  162.9 9.3 %reshape.267 = bf16[3,22,22,12,128]{4,3,2,1,0:T(8,128)(2,1)} reshape(bf16[3,22,22,1536]{3,2,1,0:T(8,128)(2,1)} %get-tuple-element.6) | data formatting | bytes 8921088 | tf_op jit(solution)/shard_map/reshape | solution.py:73
  172.2 5.8 %fusion.52 = (bf16[3,14,22,12,128]{4,3,2,1,0:T(8,128)(2,1)}, bf16[3,14,22,12,128]{4,3,2,1,0:T(8,128)(2,1)}) fusion(bf16[3,22,22,12,128]{4,3,2,1,0:T(8,128)(2,1)} %reshape.267), kind=kLoop, calls=%fused_computation.78 | loop fusion | bytes 11354112 | tf_op jit(solution)/shard_map/slice | solution.py:113
  178.0 9.3 %reshape.265 = bf16[3,22,22,12,128]{4,3,2,1,0:T(8,128)(2,1)} reshape(bf16[3,22,22,1536]{3,2,1,0:T(8,128)(2,1)} %get-tuple-element.5) | data formatting | bytes 8921088 | tf_op jit(solution)/shard_map/reshape | solution.py:74
  187.3 4.4 %fusion.51 = (bf16[3,14,22,12,128]{4,3,2,1,0:T(8,128)(2,1)S(1)}, bf16[3,14,22,12,128]{4,3,2,1,0:T(8,128)(2,1)S(1)}) fusion(bf16[3,22,22,12,128]{4,3,2,1,0:T(8,128)(2,1)} %reshape.265), kind=kLoop, calls=%fused_computation.77 | loop fusion | bytes 11354112 | tf_op jit(solution)/shard_map/slice | solution.py:114
  191.7 0.0 copy-done.3
  191.7 0.0 copy-done.4
  191.7 2.0 fusion
  193.7 1.3 fusion.2
  195.0 0.7 copy-done.2
  195.8 0.1 copy-done.5
  195.8 2.0 fusion.1
  197.8 1.3 fusion.3
  199.2 3.4 %divide_convert_fusion = (bf16[12,128,3,14,22]{1,4,3,2,0:T(8,128)(2,1)S(1)}, bf16[12,128,3,14,22]{1,4,3,2,0:T(8,128)(2,1)S(1)}) fusion(f32[12,128,3,14,22]{1,4,3,2,0:T(8,128)S(1)} %get-tuple-element.26, f32[12,128]{1,0:T(8,128)S(1)} %fusion.3, f32[12,128]{1,0:T(8,128)S(1)} %get-tuple-element.25, pred[128,3,14,22]{0,3,2,1:T(8,128)(4,1)S(1)} %get-tuple-element.18, ...), kind=kLoop, calls=%fused_computation.1 | loop fusion | flops 14192640 | bytes 17292288 | tf_op jit(solution)/shard_map/convert_element_type | solution.py:122
  202.6 0.0 slice-start.4
  202.6 2.3 %fusion.36 = bf16[12,128,128]{2,1,0:T(8,128)(2,1)S(1)} fusion(bf16[12,128,3,14,22]{1,4,3,2,0:T(8,128)(2,1)S(1)} %get-tuple-element.30, bf16[3,14,22,12,128]{4,3,2,1,0:T(8,128)(2,1)S(1)} %get-tuple-element.9), kind=kOutput, calls=%fused_computation.45 | convolution fusion | flops 363528192 | bytes 6070272 | tf_op jit(solution)/shard_map/hqtlj,tljhd->qhd/dot_general | solution.py:124
  204.9 0.0 slice-start.5
  205.0 0.0 copy-start.8
  205.0 2.3 %fusion.31 = bf16[12,128,128]{2,1,0:T(8,128)(2,1)S(1)} fusion(bf16[12,128,3,14,22]{1,4,3,2,0:T(8,128)(2,1)S(1)} %get-tuple-element.29, bf16[3,14,22,12,128]{4,3,2,1,0:T(8,128)(2,1)S(1)} %get-tuple-element.10), kind=kOutput, calls=%fused_computation.44 | convolution fusion | flops 363528192 | bytes 6070272 | tf_op jit(solution)/shard_map/hqtlj,tljhd->qhd/dot_general | solution.py:124
  207.3 2.3 %fusion.14 = bf16[256,1536]{1,0:T(8,128)(2,1)} fusion(bf16[1536,1536]{1,0:T(8,128)(2,1)S(1)} %bitcast.55, bf16[128,1536]{0,1:T(8,128)(2,1)S(1)} %bitcast.57, bf16[128,1536]{0,1:T(8,128)(2,1)S(1)} %bitcast.56, f32[1536]{0:T(1024)S(1)} %copy-done.8), kind=kOutput, calls=%fused_computation.22 | convolution fusion | flops 1210318848 | bytes 6297600 | tf_op jit(solution)/shard_map/dot_general | solution.py:129
  (28 shorter events, 0.1 us)
Async XLA Ops:
  3.5 5.6 %slice-start = ((s8[4718592]{0:T(1024)(128)(4,1)}), s8[4194304]{0:T(1024)(128)(4,1)S(1)}, s32[]{:S(2)}) async-start(s8[4718592]{0:T(1024)(128)(4,1)} %bitcast.50), calls=%async_computation | async-start | bytes 8388608
  5.2 4.0 %slice-start.1 = ((s8[4718592]{0:T(1024)(128)(4,1)}), s8[524288]{0:T(1024)(128)(4,1)S(1)}, s32[]{:S(2)}) async-start(s8[4718592]{0:T(1024)(128)(4,1)} %bitcast.50), calls=%async_computation.1 | async-start | bytes 1048576
  5.2 11.7 %slice-start.2 = ((s8[4718592]{0:T(1024)(128)(4,1)}), s8[4194304]{0:T(1024)(128)(4,1)S(1)}, s32[]{:S(2)}) async-start(s8[4718592]{0:T(1024)(128)(4,1)} %bitcast.52), calls=%async_computation.2 | async-start | bytes 8388608
  9.2 1.4 copy-start.6
  9.2 7.7 %slice-start.3 = ((s8[4718592]{0:T(1024)(128)(4,1)}), s8[524288]{0:T(1024)(128)(4,1)S(1)}, s32[]{:S(2)}) async-start(s8[4718592]{0:T(1024)(128)(4,1)} %bitcast.52), calls=%async_computation.3 | async-start | bytes 1048576
  11.0 38.0 %collective-permute-start = (bf16[1,16,16,3072]{3,2,1,0:T(8,128)(2,1)S(1)}, bf16[1,16,16,3072]{3,2,1,0:T(8,128)(2,1)S(1)}, u32[]{:S(2)}, u32[]{:S(2)}) collective-permute-start(bf16[1,16,16,3072]{3,2,1,0:T(8,128)(2,1)S(1)} %bitcast.40), channel_id=1, source_target_pairs={{0,32},{32,64},{64,96},{1,33},{33,65},{65,97},{2,34},{34,66},{66,9... | collective-permute-start | bytes 4718600 | tf_op jit(solution)/shard_map/ppermute | solution.py:18
  14.2 37.8 %collective-permute-start.1 = (bf16[1,16,16,3072]{3,2,1,0:T(8,128)(2,1)S(1)}, bf16[1,16,16,3072]{3,2,1,0:T(8,128)(2,1)S(1)}, u32[]{:S(2)}, u32[]{:S(2)}) collective-permute-start(bf16[1,16,16,3072]{3,2,1,0:T(8,128)(2,1)S(1)} %bitcast.41), channel_id=1, source_target_pairs={{32,0},{64,32},{96,64},{33,1},{65,33},{97,65},{34,2},{66,34},{98,6... | collective-permute-start | bytes 4718600 | tf_op jit(solution)/shard_map/ppermute | solution.py:20
  18.4 37.1 %copy-start.7 = (f32[1536]{0:T(1024)S(1)}, f32[1536]{0:T(1024)}, u32[]{:S(2)}) copy-start(f32[1536]{0:T(1024)} %param.18) | copy-start | bytes 18436
  52.0 1.7 copy-start
  53.7 20.4 %collective-permute-start.2 = (bf16[3,3,16,3072]{3,2,1,0:T(8,128)(2,1)}, bf16[3,3,16,3072]{3,2,1,0:T(8,128)(2,1)}, u32[]{:S(2)}, u32[]{:S(2)}) collective-permute-start(bf16[3,3,16,3072]{3,2,1,0:T(8,128)(2,1)} %get-tuple-element.13), channel_id=1, source_target_pairs={{0,8},{8,16},{16,24},{24,0},{1,9},{9,17},{17,25},{25,1},{2,10},{10... | collective-permute-start | bytes 2654216 | tf_op jit(solution)/shard_map/ppermute | solution.py:18
  53.7 21.3 %collective-permute-start.3 = (bf16[3,3,16,3072]{3,2,1,0:T(8,128)(2,1)}, bf16[3,3,16,3072]{3,2,1,0:T(8,128)(2,1)}, u32[]{:S(2)}, u32[]{:S(2)}) collective-permute-start(bf16[3,3,16,3072]{3,2,1,0:T(8,128)(2,1)} %get-tuple-element.14), channel_id=1, source_target_pairs={{8,0},{16,8},{24,16},{0,24},{9,1},{17,9},{25,17},{1,25},{10,2},{18... | collective-permute-start | bytes 2654216 | tf_op jit(solution)/shard_map/ppermute | solution.py:20
  79.3 35.9 %collective-permute-start.4 = (bf16[3,22,3,3072]{3,1,2,0:T(8,128)(2,1)S(1)}, bf16[3,22,3,3072]{3,1,2,0:T(8,128)(2,1)S(1)}, u32[]{:S(2)}, u32[]{:S(2)}) collective-permute-start(bf16[3,22,3,3072]{3,1,2,0:T(8,128)(2,1)S(1)} %copy.36), channel_id=1, source_target_pairs={{0,1},{1,2},{2,3},{3,4},{4,5},{5,6},{6,7},{7,0},{8,9},{9,10},{10,1... | collective-permute-start | bytes 3649544 | tf_op jit(solution)/shard_map/ppermute | solution.py:18
  82.5 61.0 %copy-start.1 = (bf16[1,16,16,3072]{3,2,1,0:T(8,128)(2,1)S(1)}, bf16[1,16,16,3072]{3,2,1,0:T(8,128)(2,1)}, u32[]{:S(2)}) copy-start(bf16[1,16,16,3072]{3,2,1,0:T(8,128)(2,1)} %copy-done) | copy-start | bytes 4718596
  82.5 59.9 %collective-permute-start.5 = (bf16[3,22,3,3072]{3,1,2,0:T(8,128)(2,1)S(1)}, bf16[3,22,3,3072]{3,1,2,0:T(8,128)(2,1)S(1)}, u32[]{:S(2)}, u32[]{:S(2)}) collective-permute-start(bf16[3,22,3,3072]{3,1,2,0:T(8,128)(2,1)S(1)} %copy.37), channel_id=1, source_target_pairs={{1,0},{2,1},{3,2},{4,3},{5,4},{6,5},{7,6},{0,7},{9,8},{10,9},{11,1... | collective-permute-start | bytes 3649544 | tf_op jit(solution)/shard_map/ppermute | solution.py:20
  187.3 4.4 %copy-start.3 = (bf16[3,14,22,12,128]{4,3,2,1,0:T(8,128)(2,1)S(1)}, bf16[3,14,22,12,128]{4,3,2,1,0:T(8,128)(2,1)}, u32[]{:S(2)}) copy-start(bf16[3,14,22,12,128]{4,3,2,1,0:T(8,128)(2,1)} %get-tuple-element.11) | copy-start | bytes 8515588
  187.3 4.4 %copy-start.4 = (bf16[1,8,16,12,128]{4,2,1,3,0:T(8,128)(2,1)S(1)}, bf16[1,8,16,12,128]{4,2,1,3,0:T(8,128)(2,1)}, u32[]{:S(2)}) copy-start(bf16[1,8,16,12,128]{4,2,1,3,0:T(8,128)(2,1)} %copy.41) | copy-start | bytes 1179652
  193.7 2.1 copy-start.2
  193.7 2.1 %copy-start.5 = (bf16[1,8,16,12,128]{4,2,1,3,0:T(8,128)(2,1)S(1)}, bf16[1,8,16,12,128]{4,2,1,3,0:T(8,128)(2,1)}, u32[]{:S(2)}) copy-start(bf16[1,8,16,12,128]{4,2,1,3,0:T(8,128)(2,1)} %copy.45) | copy-start | bytes 1179652
  202.6 4.7 %slice-start.4 = ((s8[4718592]{0:T(1024)(128)(4,1)}), s8[4194304]{0:T(1024)(128)(4,1)S(1)}, s32[]{:S(2)}) async-start(s8[4718592]{0:T(1024)(128)(4,1)} %bitcast.54), calls=%async_computation.4 | async-start | bytes 8388608
  204.9 2.4 %slice-start.5 = ((s8[4718592]{0:T(1024)(128)(4,1)}), s8[524288]{0:T(1024)(128)(4,1)S(1)}, s32[]{:S(2)}) async-start(s8[4718592]{0:T(1024)(128)(4,1)} %bitcast.54), calls=%async_computation.5 | async-start | bytes 1048576
  205.0 2.4 %copy-start.8 = (f32[1536]{0:T(1024)S(1)}, f32[1536]{0:T(1024)}, u32[]{:S(2)}) copy-start(f32[1536]{0:T(1024)} %param.13) | copy-start | bytes 18436
where the time goes:
time: 212 us; the launch traced here: 210 us
  waiting for transfers between devices  99.5 us (47%)
  local copies, waits for them, and re-layouts  48.6 us (23%)
  other arithmetic  29.3 us (14%)
  matrix products  17.7 us (8%)
  starting transfers between devices  14.1 us (7%)
    ppermute x3, waiting for transfers between devices, padded(): lax.ppermute(tail, axis, [(i, (i + 1) % count) for i in range(ends)])  69.5 us
    ppermute x3, waiting for transfers between devices, padded(): lax.ppermute(head, axis, [((i + 1) % count, i) for i in range(ends)])  30 us
    concatenate x1, other arithmetic, padded(): jnp.concatenate([lax.ppermute(tail, axis, [(i, (i + 1) % count) for i in...  11 us
    reshape x1, local copies, waits for them, and re-layouts, shards(): key_grid = widened[..., :model_width].reshape(head_shape)  9.31 us
    reshape x1, local copies, waits for them, and re-layouts, shards(): value_grid = widened[..., model_width:].reshape(head_shape)  9.31 us
    slice x1, local copies, waits for them, and re-layouts, shards(): value_grid = widened[..., model_width:].reshape(head_shape)  8.39 us
    ppermute x3, starting transfers between devices, padded(): lax.ppermute(head, axis, [((i + 1) % count, i) for i in range(ends)])  8.13 us
    ppermute x3, starting transfers between devices, padded(): lax.ppermute(tail, axis, [(i, (i + 1) % count) for i in range(ends)])  5.99 us
  transfers between devices with their start and end apart: 6, of which 6 were waited for; matrix products, arithmetic and copies ran while one was open for 6% of the time, Pallas kernels for 0%

commit v1 on v0

v1 whole, which is shorter than its diff:
```python
import functools
import math

import jax
import jax.numpy as jnp
import numpy as np
from jax import lax
from jax.experimental import pallas as pl
from jax.experimental.pallas import tpu as pltpu
from jax.sharding import PartitionSpec as P

HEADS = 12
HEAD_DIM = 128
D = 1536
SIDE = 16
TOKENS = SIDE * SIDE
KEYS = 1536
BF = jnp.bfloat16
F32 = jnp.float32
MESH = pl.DeviceIdType.MESH
MASKED = -1e30
SCALE = HEAD_DIM ** (-0.5) * math.log2(math.e)

OWN = 0
OWN_HALO = 256
C1 = (512, 608)
C2 = (704, 768)
C3 = (832, 928)
HALOS = (1024, 1280)
HALO_AT = (OWN_HALO, HALOS[0], HALOS[1])
CHUNKS = ((0, 96), (96, 64), (160, 96))
PIECES = ((0, 48), (48, 48), (96, 48), (144, 48), (192, 16), (208, 16), (224, 16), (240, 16))


def center_order():
    order = [(r, c) for c in (0, 1, 2, 13, 14, 15) for r in range(16)]
    order += [(r, c) for r in (0, 1, 2) for c in range(3, 13)]
    order += [(r, c) for r in (13, 14, 15) for c in range(3, 13)]
    order += [(r, c) for r in range(3, 13) for c in range(3, 13)]
    return order


def edge_lists():
    lo, hi, full = (0, 1, 2), (13, 14, 15), range(16)
    north = [(r, c) for r in lo for c in full]
    south = [(r, c) for r in hi for c in full]
    corners = []
    for rows in (lo, hi):
        for cols in (lo, hi):
            corners.append([(r, c) for r in rows for c in cols] + [None] * 7)
    return north, south, corners


def tables():
    order = center_order()
    where = {p: i for i, p in enumerate(order)}
    perm = np.zeros((TOKENS, TOKENS), np.float32)
    for i, (r, c) in enumerate(order):
        perm[i, r * SIDE + c] = 1
    north, south, corners = edge_lists()
    pack_list = north + south + sum(corners, [])
    pack = np.zeros((160, 160), np.float32)
    for i, p in enumerate(pack_list):
        if p is not None:
            pack[i, where[p]] = 1

    def moved(cells, dr, dc):
        return [None if p is None else (p[0] + dr, p[1] + dc) for p in cells]

    lo = [(r, c) for c in (0, 1, 2) for r in range(16)]
    hi = [(r, c) for c in (13, 14, 15) for r in range(16)]
    nw, ne, sw, se = corners
    halo = moved(hi, 0, -16) + moved(lo, 0, 16) + moved(south, -16, 0) + moved(north, 16, 0)
    halo += moved(se, -16, -16) + moved(sw, -16, 16) + moved(ne, 16, -16) + moved(nw, 16, 16)
    keys = order + halo
    for a, n in CHUNKS:
        keys += order[a : a + n] * 2
    keys += halo * 2
    bias = np.full((TOKENS, KEYS), MASKED, np.float32)
    for j, p in enumerate(keys):
        if p is None:
            continue
        for i, (r, c) in enumerate(order):
            if abs(r - p[0]) <= 3 and abs(c - p[1]) <= 3:
                bias[i, j] = 0
    return perm, perm.T.copy(), pack, bias


def kernel(
    x_ref, shift_ref, scale_ref, gate_ref, qgain_ref, kgain_ref, wq_any, wk_any, wv_any, wo_any,
    perm_ref, back_ref, pack_ref, bias_ref, out_ref,
    wq, wk, wv, wo, xs, ks, vs, qs, packed, flat, bias, acc, m_ref, l_ref,
    w_sem, y_send, y_recv, h_send, h_recv,
):
    t, a, o = lax.axis_index("tm"), lax.axis_index("lat"), lax.axis_index("lon")
    west, east = lax.rem(o + 7, 8), lax.rem(o + 1, 8)
    has_prev, has_next = t > 0, t < 3
    has_north, has_south = a > 0, a < 3
    dirs = (
        (None, (t, a, west)), (None, (t, a, east)),
        (has_north, (t, a - 1, o)), (has_south, (t, a + 1, o)),
        (has_north, (t, a - 1, west)), (has_north, (t, a - 1, east)),
        (has_south, (t, a + 1, west)), (has_south, (t, a + 1, east)),
    )
    opposite = (1, 0, 3, 2, 7, 6, 5, 4)
    frames = ((has_prev, (t - 1, a, o)), (has_next, (t + 1, a, o)))

    def when(cond, fn):
        if cond is None:
            fn()
        else:
            pl.when(cond)(fn)

    loads = []
    for i, (src, dst) in enumerate(((wq_any, wq), (wk_any, wk), (wv_any, wv), (wo_any, wo))):
        loads.append(pltpu.make_async_copy(src, dst, w_sem.at[i]))
        loads[-1].start()

    barrier = pltpu.get_barrier_semaphore()
    for cond, dev in dirs + frames:
        when(cond, lambda dev=dev: pl.semaphore_signal(barrier, inc=1, device_id=dev, device_id_type=MESH))

    one = lambda c: jnp.where(c, 1, 0)

    @pl.loop(0, 4)
    def _(i):
        rows = pl.ds(pl.multiple_of(i * 64, 64), 64)
        v = x_ref[rows, :].astype(F32)
        centred = v - jnp.mean(v, axis=-1, keepdims=True)
        var = jnp.mean(centred * centred, axis=-1, keepdims=True)
        flat[rows, :] = (centred * lax.rsqrt(var + 1e-06) * (1.0 + scale_ref[...]) + shift_ref[...]).astype(BF)

    xs[0:TOKENS, :] = jnp.dot(perm_ref[...], flat[...], preferred_element_type=F32).astype(BF)
    pl.semaphore_wait(barrier, 2 + one(has_prev) + one(has_next) + 3 * one(has_north) + 3 * one(has_south))

    def y_copy(chunk, side):
        start, n = CHUNKS[chunk]
        dst = (C1, C2, C3)[chunk][1 - side]
        return pltpu.make_async_remote_copy(
            src_ref=xs.at[start : start + n], dst_ref=xs.at[dst : dst + n],
            send_sem=y_send.at[chunk, side], recv_sem=y_recv.at[chunk, 1 - side],
            device_id=frames[side][1], device_id_type=MESH,
        )

    def y_start(chunk):
        for side in range(2):
            when(frames[side][0], lambda side=side: y_copy(chunk, side).start())

    def y_arrived(chunk, slot):
        start, n = CHUNKS[chunk]
        dst = (C1, C2, C3)[chunk][slot]
        return pltpu.make_async_remote_copy(
            src_ref=xs.at[dst : dst + n], dst_ref=xs.at[dst : dst + n],
            send_sem=y_send.at[chunk, slot], recv_sem=y_recv.at[chunk, slot],
            device_id=frames[slot][1], device_id_type=MESH,
        )

    def h_copy(slot, d):
        off, n = PIECES[opposite[d]]
        dst = HALO_AT[slot] + off
        if d < 2:
            base = (OWN, C1[0], C1[1])[slot] + 48 * d
            src = xs.at[base : base + 48]
        else:
            so = PIECES[d][0] - 96
            src = packed.at[slot, so : so + n]
        return pltpu.make_async_remote_copy(
            src_ref=src, dst_ref=xs.at[dst : dst + n],
            send_sem=h_send.at[slot, d], recv_sem=h_recv.at[slot, opposite[d]],
            device_id=dirs[d][1], device_id_type=MESH,
        )

    def h_arrived(slot, d):
        off, n = PIECES[d]
        dst = HALO_AT[slot] + off
        return pltpu.make_async_remote_copy(
            src_ref=xs.at[dst : dst + n], dst_ref=xs.at[dst : dst + n],
            send_sem=h_send.at[slot, d], recv_sem=h_recv.at[slot, d],
            device_id=dirs[d][1], device_id_type=MESH,
        )

    def h_start(slot, which):
        for d in which:
            when(dirs[d][0], lambda d=d: h_copy(slot, d).start())

    def h_wait(slot, which):
        for d in which:
            when(dirs[d][0], lambda d=d: h_arrived(slot, d).wait_recv())

    def pack(slot):
        if slot == 0:
            edge = xs[0:160, :]
        else:
            b, c = C1[slot - 1], C2[slot - 1]
            edge = jnp.concatenate([xs[b : b + 96, :], xs[c : c + 64, :]], axis=0)
        packed[slot] = jnp.dot(pack_ref[...], edge, preferred_element_type=F32).astype(BF)

    y_start(0)
    h_start(0, (0, 1))
    y_start(1)
    pack(0)
    h_start(0, range(2, 8))
    y_start(2)

    def clear(start, n):
        xs[start : start + n, :] = jnp.zeros((n, D), BF)

    for slot in range(2):
        def absent(slot=slot):
            for (_, n), c in zip(CHUNKS, (C1, C2, C3)):
                clear(c[slot], n)
            clear(HALOS[slot], 256)
        pl.when(jnp.logical_not(frames[slot][0]))(absent)
    for cond, pieces in ((has_north, (2, 4, 5)), (has_south, (3, 6, 7))):
        def edge_clear(pieces=pieces):
            for slot in range(3):
                present = None if slot == 0 else frames[slot - 1][0]
                for d in pieces:
                    off, n = PIECES[d]
                    when(present, lambda off=off, n=n, slot=slot: clear(HALO_AT[slot] + off, n))
        pl.when(jnp.logical_not(cond))(edge_clear)

    j = lax.broadcasted_iota(jnp.int32, (1, KEYS), 1)
    extra = jnp.zeros((1, KEYS), F32)

    def bar(extra, cond, start, n):
        off = (j >= start) & (j < start + n) & jnp.logical_not(cond)
        return jnp.where(off, MASKED, extra)

    for slot in range(2):
        for (_, n), c in zip(CHUNKS, (C1, C2, C3)):
            extra = bar(extra, frames[slot][0], c[slot], n)
        extra = bar(extra, frames[slot][0], HALOS[slot], 256)
    for base in HALO_AT:
        for cond, pieces in ((has_north, (2, 4, 5)), (has_south, (3, 6, 7))):
            for d in pieces:
                extra = bar(extra, cond, base + PIECES[d][0], PIECES[d][1])
    bias[...] = jnp.minimum(bias_ref[...].astype(F32), extra)

    def rms(p, gain):
        ms = jnp.mean(p * p, axis=-1, keepdims=True)
        return (p * lax.rsqrt(ms + 1e-06) * gain).astype(BF)

    def keys_of(start, n):
        p = jnp.dot(xs[start : start + n, :], wk[...], preferred_element_type=F32)
        ks[start : start + n, :] = rms(p, kgain_ref[...])

    def values_of(start, n):
        vs[start : start + n, :] = jnp.dot(
            xs[start : start + n, :], wv[...], preferred_element_type=F32
        ).astype(BF)

    def attend(start, n, first):
        @pl.loop(0, HEADS)
        def _(h):
            hs = pl.ds(pl.multiple_of(h * HEAD_DIM, HEAD_DIM), HEAD_DIM)
            s = lax.dot_general(
                qs[:, hs], ks[start : start + n, hs], (((1,), (1,)), ((), ())), preferred_element_type=F32
            )
            s = s * SCALE + bias[:, start : start + n]
            m = jnp.max(s, axis=-1, keepdims=True)
            if not first:
                old = m_ref[h]
                m = jnp.maximum(m, old)
            p = jnp.exp2(s - m)
            l = jnp.sum(p, axis=-1, keepdims=True)
            pv = jnp.dot(p.astype(BF), vs[start : start + n, hs], preferred_element_type=F32)
            if not first:
                alpha = jnp.exp2(old - m)
                l = l + alpha * l_ref[h]
                pv = pv + alpha * acc[:, hs]
            m_ref[h] = m
            l_ref[h] = l
            acc[:, hs] = pv

    loads[0].wait()
    qs[...] = rms(jnp.dot(xs[0:TOKENS, :], wq[...], preferred_element_type=F32), qgain_ref[...])
    loads[1].wait()
    keys_of(0, TOKENS)
    loads[2].wait()
    values_of(0, TOKENS)

    for slot in range(2):
        def forward(slot=slot):
            y_arrived(0, slot).wait_recv()
            h_start(slot + 1, (0, 1))
        pl.when(frames[slot][0])(forward)
    h_wait(0, range(8))
    keys_of(256, 448)
    for slot in range(2):
        def forward(slot=slot):
            y_arrived(1, slot).wait_recv()
            pack(slot + 1)
            h_start(slot + 1, range(2, 8))
        pl.when(frames[slot][0])(forward)
    values_of(256, 448)
    attend(0, 512, True)
    for slot in range(2):
        pl.when(frames[slot][0])(lambda slot=slot: y_arrived(2, slot).wait_recv())
    pl.when(has_prev)(lambda: h_wait(1, range(8)))
    keys_of(704, 576)
    values_of(704, 576)
    attend(512, 768, False)
    pl.when(has_next)(lambda: h_wait(2, range(8)))
    keys_of(1280, 256)
    values_of(1280, 256)
    attend(1280, 256, False)

    @pl.loop(0, HEADS)
    def _(h):
        hs = pl.ds(pl.multiple_of(h * HEAD_DIM, HEAD_DIM), HEAD_DIM)
        qs[:, hs] = (acc[:, hs] / l_ref[h]).astype(BF)

    flat[...] = jnp.dot(back_ref[...], qs[...], preferred_element_type=F32).astype(BF)
    loads[3].wait()
    out_ref[...] = (jnp.dot(flat[...], wo[...], preferred_element_type=F32) * gate_ref[...]).astype(BF)

    for chunk in range(3):
        for side in range(2):
            when(frames[side][0], lambda chunk=chunk, side=side: y_copy(chunk, side).wait_send())
    for slot in range(3):
        present = None if slot == 0 else frames[slot - 1][0]
        for d in range(8):
            def done(slot=slot, d=d):
                when(dirs[d][0], lambda: h_copy(slot, d).wait_send())
            when(present, done)


def shards(latents, ada_shift, ada_scale, ada_gate, w_query, w_key, w_value, w_out, query_gain, key_gain):
    perm, back, pack, bias = tables()
    row = lambda v: v.reshape(1, D)
    vmem = pl.BlockSpec(memory_space=pltpu.VMEM)
    hbm = pl.BlockSpec(memory_space=pl.ANY)
    out = pl.pallas_call(
        kernel,
        out_shape=jax.ShapeDtypeStruct((TOKENS, D), BF),
        in_specs=[vmem] * 6 + [hbm] * 4 + [vmem] * 4,
        out_specs=vmem,
        scratch_shapes=[pltpu.VMEM((D, D), BF)] * 4
        + [
            pltpu.VMEM((KEYS, D), BF),
            pltpu.VMEM((KEYS, D), BF),
            pltpu.VMEM((KEYS, D), BF),
            pltpu.VMEM((TOKENS, D), BF),
            pltpu.VMEM((3, 160, D), BF),
            pltpu.VMEM((TOKENS, D), BF),
            pltpu.VMEM((TOKENS, KEYS), F32),
            pltpu.VMEM((TOKENS, D), F32),
            pltpu.VMEM((HEADS, TOKENS, 1), F32),
            pltpu.VMEM((HEADS, TOKENS, 1), F32),
            pltpu.SemaphoreType.DMA((4,)),
            pltpu.SemaphoreType.DMA((3, 2)),
            pltpu.SemaphoreType.DMA((3, 2)),
            pltpu.SemaphoreType.DMA((3, 8)),
            pltpu.SemaphoreType.DMA((3, 8)),
        ],
        compiler_params=pltpu.CompilerParams(
            collective_id=0, has_side_effects=True, vmem_limit_bytes=60 * 2**20
        ),
        cost_estimate=pl.CostEstimate(flops=2 * 10**10, bytes_accessed=2 * 10**7, transcendentals=5 * 10**6),
    )(
        latents.reshape(TOKENS, D), row(ada_shift), row(ada_scale), row(ada_gate), row(query_gain), row(key_gain),
        w_query, w_key, w_value, w_out,
        jnp.asarray(perm, BF), jnp.asarray(back, BF), jnp.asarray(pack, BF), jnp.asarray(bias, BF),
    )
    return out.reshape(latents.shape)


def solution(mesh):
    return jax.shard_map(
        shards,
        mesh=mesh,
        in_specs=(P("tm", "lat", "lon", None),) + (P(),) * 9,
        out_specs=P("tm", "lat", "lon", None),
        check_vma=False,
    )
```

time: 212 us -> 75 us (0.35)
  waiting for transfers between devices: 99.5 us -> 0 us
  Pallas kernels: 0 us -> 66.1 us
  local copies, waits for them, and re-layouts: 48.6 us -> 8.52 us
  other arithmetic: 29.3 us -> 0 us
  matrix products: 17.7 us -> 0 us
  starting transfers between devices: 14.1 us -> 0 us
    ppermute x6 -> x0, waiting for transfers between devices: 99.5 us -> none  [the longest x3 69.5 us: padded(): lax.ppermute(tail, axis, [(i, (i + 1) % count) for i in range(ends)])]
    pallas_call x0 -> x1, Pallas kernels: none -> 66.1 us  [shards(): pl.pallas_call(kernel, out_shape=jax.ShapeDtypeStruct((TOKENS, D), BF), i...]
    slice x8 -> x0, local copies, waits for them, and re-layouts: 24.4 us -> none  [the longest x1 8.39 us: shards(): value_grid = widened[..., model_width:].reshape(head_shape)]
    dot_general x8 -> x0, matrix products: 17.7 us -> none  [the longest x2 4.63 us: shards(): jnp.einsum('hqtlj,tljhd->qhd', probs, value_block, preferred_element_type...]
    reshape x3 -> x5, local copies, waits for them, and re-layouts: 21 us -> 6.46 us  [shards(): row = lambda v: v.reshape(1, D)]
    ppermute x6 -> x0, starting transfers between devices: 14.1 us -> none  [the longest x3 8.13 us: padded(): lax.ppermute(head, axis, [((i + 1) % count, i) for i in range(ends)])]
    concatenate x2 -> x0, other arithmetic: 11.1 us -> none  [the longest x1 11 us: padded(): jnp.concatenate([lax.ppermute(tail, axis, [(i, (i + 1) % count) for i in...]
    convert_element_type x4 -> x0, other arithmetic: 6.33 us -> none  [the longest x1 3.42 us: shards(): (raw_weights / jnp.sum(raw_weights, axis=-1, keepdims=True)).astype(jnp.b...]
  transfers between devices with their start and end apart: 6 -> 0, of which waited for: 6 -> 0; matrix products, arithmetic and copies ran while one was open for 6% -> 0% of each run, Pallas kernels for 0% -> 0%
where the time goes in v1:
time: 75 us; the launch traced here: 74.7 us
  Pallas kernels  66.1 us (88%)
  local copies, waits for them, and re-layouts  8.52 us (11%)
    pallas_call x1, Pallas kernels, shards(): pl.pallas_call(kernel, out_shape=jax.ShapeDtypeStruct((TOKENS, D), BF), i...  66.1 us
    reshape x5, local copies, waits for them, and re-layouts, shards(): row = lambda v: v.reshape(1, D)  6.46 us
    unnamed x1, local copies, waits for them, and re-layouts  2.06 us

profile of v1, /device:TPU:16, one launch (start us, length us, event | category | flops | bytes accessed | tf_op | source)
XLA Modules:
  0.0 74.7 jit_solution(18214466549122866160)
XLA Ops:
  0.0 1.3 %reshape.22.shift_ref = f32[1,1536]{1,0:T(1,128)} reshape(f32[1536]{0:T(1024)} %param.15) | data formatting | bytes 12288 | tf_op jit(solution)/shard_map/reshape | solution.py:331
  1.3 1.3 %reshape.23.scale_ref = f32[1,1536]{1,0:T(1,128)} reshape(f32[1536]{0:T(1024)} %param.16) | data formatting | bytes 12288 | tf_op jit(solution)/shard_map/reshape | solution.py:331
  2.6 1.3 %reshape.24.gate_ref = f32[1,1536]{1,0:T(1,128)} reshape(f32[1536]{0:T(1024)} %param.17) | data formatting | bytes 12288 | tf_op jit(solution)/shard_map/reshape | solution.py:331
  3.9 1.3 %reshape.25.qgain_ref = f32[1,1536]{1,0:T(1,128)} reshape(f32[1536]{0:T(1024)} %param.22) | data formatting | bytes 12288 | tf_op jit(solution)/shard_map/reshape | solution.py:331
  5.2 1.3 %reshape.26.kgain_ref = f32[1,1536]{1,0:T(1,128)} reshape(f32[1536]{0:T(1024)} %param.23) | data formatting | bytes 12288 | tf_op jit(solution)/shard_map/reshape | solution.py:331
  6.5 66.1 %shard_map.136 = bf16[256,1536]{1,0:T(8,128)(2,1)} custom-call(bf16[256,1536]{1,0:T(8,128)(2,1)} %bitcast.3, f32[1,1536]{1,0:T(1,128)} %reshape.22.shift_ref, f32[1,1536]{1,0:T(1,128)} %reshape.23.scale_ref, f32[1,1536]{1,0:T(1,128)} %reshape.24.gate_ref, f32[1,1536]{1,0:T(1,128)} %reshape.25.qgain_ref, f32[1,1536]{1,0:T(1,128)} %reshape.26.kgain_ref, ...), custom_call_target="tpu_custom_call" | custom-call | flops 20000000000 | bytes 20000000 | tf_op jit(solution)/shard_map/pallas_call | solution.py:334
  72.6 2.1 %copy.16 = bf16[1,16,16,1536]{3,2,1,0:T(8,128)(2,1)} copy(bf16[1,16,16,1536]{3,2,1,0:T(8,128)(2,1)} %bitcast.2) | data formatting | bytes 1572864

commit v2 on v1

v2 whole, which is shorter than its diff:
```python
import functools
import math

import jax
import jax.numpy as jnp
import numpy as np
from jax import lax
from jax.experimental import pallas as pl
from jax.experimental.pallas import tpu as pltpu
from jax.sharding import PartitionSpec as P

HEADS = 12
HEAD_DIM = 128
D = 1536
SIDE = 16
TOKENS = SIDE * SIDE
KEYS = 1536
BF = jnp.bfloat16
F32 = jnp.float32
MESH = pl.DeviceIdType.MESH
MASKED = -1e30
GROUP = 4
SCALE = HEAD_DIM ** (-0.5) * math.log2(math.e)

CHUNKS = ((0, 48), (48, 112), None, (160, 96))
CHUNK_ROWS = (48, 112, 48, 96)
CHUNK_AT = ((512, 560), (608, 720), (832, 880), (1024, 1120))
HALO_E = 304
WEST_AT = (256, 928, 976)
ROWS_AT = (352, 1216, 1376)


def center_order():
    order = [(r, c) for c in (13, 14, 15, 0, 1, 2) for r in range(16)]
    order += [(r, c) for r in (0, 1, 2) for c in range(3, 13)]
    order += [(r, c) for r in (13, 14, 15) for c in range(3, 13)]
    order += [(r, c) for r in range(3, 13) for c in range(3, 13)]
    return order


def tables():
    order = center_order()
    natural = [(r, c) for r in range(SIDE) for c in range(SIDE)]
    west = [(r, c - 16) for c in (13, 14, 15) for r in range(16)]
    east = [(r, c + 16) for c in (0, 1, 2) for r in range(16)]
    bands = [[(r, c) for r in rows for c in range(-3, 19)] + [None] * 14 for rows in ((0, 1, 2), (13, 14, 15))]
    north = [p and (p[0] - 16, p[1]) for p in bands[1]]
    south = [p and (p[0] + 16, p[1]) for p in bands[0]]
    select = np.zeros((TOKENS, TOKENS), np.float32)
    for i, (r, c) in enumerate(order):
        select[i, r * SIDE + c] = 1
    where = {p: i for i, p in enumerate(order[:160] + west + east)}
    pack = np.zeros((160, 256), np.float32)
    for i, p in enumerate(bands[0] + bands[1]):
        if p is not None:
            pack[i, where[p]] = 1
    keys = [None] * KEYS

    def place(start, cells):
        keys[start : start + len(cells)] = cells

    place(0, natural)
    place(HALO_E, east)
    for chunk, spots in zip(CHUNKS, CHUNK_AT):
        for spot in spots:
            place(spot, order[chunk[0] : sum(chunk)] if chunk else east)
    for slot in range(3):
        place(WEST_AT[slot], west)
        place(ROWS_AT[slot], north + south)
    bias = np.full((TOKENS, KEYS), MASKED, np.float32)
    for j, p in enumerate(keys):
        if p is None:
            continue
        for i, (r, c) in enumerate(natural):
            if abs(r - p[0]) <= 3 and abs(c - p[1]) <= 3:
                bias[i, j] = 0
    return select, pack, bias


def kernel(
    x_ref, shift_ref, scale_ref, gate_ref, qgain_ref, kgain_ref, wq_any, wk_any, wv_any, wo_any,
    select_ref, pack_ref, bias_any, out_ref,
    wq, wk, wv, wo, xs, ks, vs, qs, staged, packed, bias_in, bias, acc, m_ref, l_ref, score, prob, new_m, new_l,
    w_sem, y_send, y_recv, h_send, h_recv,
):
    t, a, o = lax.axis_index("tm"), lax.axis_index("lat"), lax.axis_index("lon")
    west, east = lax.rem(o + 7, 8), lax.rem(o + 1, 8)
    has_prev, has_next = t > 0, t < 3
    has_north, has_south = a > 0, a < 3
    dirs = (
        (None, (t, a, west)), (None, (t, a, east)),
        (has_north, (t, a - 1, o)), (has_south, (t, a + 1, o)),
    )
    opposite = (1, 0, 3, 2)
    frames = ((has_prev, (t - 1, a, o)), (has_next, (t + 1, a, o)))

    def when(cond, fn):
        if cond is None:
            fn()
        else:
            pl.when(cond)(fn)

    loads = []
    pairs = ((wq_any, wq), (wk_any, wk), (bias_any, bias_in), (wv_any, wv), (wo_any, wo))
    for i, (src, dst) in enumerate(pairs):
        loads.append(pltpu.make_async_copy(src, dst, w_sem.at[i]))
        loads[-1].start()

    barrier = pltpu.get_barrier_semaphore()
    for cond, dev in dirs + frames:
        when(cond, lambda dev=dev: pl.semaphore_signal(barrier, inc=1, device_id=dev, device_id_type=MESH))

    one = lambda c: jnp.where(c, 1, 0)

    row = lambda ref: ref[...].reshape(1, D)
    shift, scale = row(shift_ref), 1.0 + row(scale_ref)

    @pl.loop(0, 8)
    def _(i):
        rows = pl.ds(pl.multiple_of(i * 32, 32), 32)
        v = x_ref[rows, :].astype(F32)
        centred = v - jnp.mean(v, axis=-1, keepdims=True)
        var = jnp.mean(centred * centred, axis=-1, keepdims=True)
        xs[rows, :] = (centred * lax.rsqrt(var + 1e-06) * scale + shift).astype(BF)

    staged[...] = jnp.dot(select_ref[...], xs[0:TOKENS, :], preferred_element_type=F32).astype(BF)
    pl.semaphore_wait(barrier, 2 + one(has_prev) + one(has_next) + one(has_north) + one(has_south))

    def y_copy(chunk, side):
        n, dst = CHUNK_ROWS[chunk], CHUNK_AT[chunk][1 - side]
        if CHUNKS[chunk]:
            src = staged.at[CHUNKS[chunk][0] : sum(CHUNKS[chunk])]
        else:
            src = xs.at[HALO_E : HALO_E + n]
        return pltpu.make_async_remote_copy(
            src_ref=src, dst_ref=xs.at[dst : dst + n],
            send_sem=y_send.at[chunk, side], recv_sem=y_recv.at[chunk, 1 - side],
            device_id=frames[side][1], device_id_type=MESH,
        )

    def y_start(chunk):
        for side in range(2):
            when(frames[side][0], lambda side=side: y_copy(chunk, side).start())

    def y_arrived(chunk, slot):
        n, dst = CHUNK_ROWS[chunk], CHUNK_AT[chunk][slot]
        return pltpu.make_async_remote_copy(
            src_ref=xs.at[dst : dst + n], dst_ref=xs.at[dst : dst + n],
            send_sem=y_send.at[chunk, slot], recv_sem=y_recv.at[chunk, slot],
            device_id=frames[slot][1], device_id_type=MESH,
        )

    def piece(slot, d):
        if d == 0:
            return WEST_AT[slot], 48
        if d == 1:
            return HALO_E, 48
        return ROWS_AT[slot] + 80 * (d - 2), 80

    def h_copy(slot, d):
        dst, n = piece(slot, opposite[d])
        if d >= 2:
            src = packed.at[slot, 80 * (d - 2) : 80 * (d - 1)]
        elif slot == 0:
            src = staged.at[48 - 48 * d : 96 - 48 * d]
        else:
            src = xs.at[CHUNK_AT[0][slot - 1] : CHUNK_AT[0][slot - 1] + 48]
        return pltpu.make_async_remote_copy(
            src_ref=src, dst_ref=xs.at[dst : dst + n],
            send_sem=h_send.at[slot, d], recv_sem=h_recv.at[slot, opposite[d]],
            device_id=dirs[d][1], device_id_type=MESH,
        )

    def h_arrived(slot, d):
        dst, n = piece(slot, d)
        return pltpu.make_async_remote_copy(
            src_ref=xs.at[dst : dst + n], dst_ref=xs.at[dst : dst + n],
            send_sem=h_send.at[slot, d], recv_sem=h_recv.at[slot, d],
            device_id=dirs[d][1], device_id_type=MESH,
        )

    def h_start(slot, which):
        for d in which:
            when(dirs[d][0], lambda d=d: h_copy(slot, d).start())

    def h_wait(slot, which):
        for d in which:
            when(dirs[d][0], lambda d=d: h_arrived(slot, d).wait_recv())

    def y_sent(chunk):
        for side in range(2):
            when(frames[side][0], lambda side=side: y_copy(chunk, side).wait_send())

    def h_sent(slot, which):
        for d in which:
            when(dirs[d][0], lambda d=d: h_copy(slot, d).wait_send())

    def pack(slot):
        if slot == 0:
            parts = [staged[0:160, :], xs[256:352, :]]
        else:
            spots = [(CHUNK_AT[k][slot - 1], CHUNK_ROWS[k]) for k in range(3)]
            spots.insert(2, (WEST_AT[slot], 48))
            parts = [xs[p : p + n, :] for p, n in spots]
        edge = jnp.concatenate(parts, axis=0)
        packed[slot] = jnp.dot(pack_ref[...], edge, preferred_element_type=F32).astype(BF)

    y_start(0)
    h_start(0, (0, 1))

    def clear(start, n):
        xs[start : start + n, :] = jnp.zeros((n, D), BF)

    for slot in range(2):
        def absent(slot=slot):
            for n, c in zip(CHUNK_ROWS, CHUNK_AT):
                clear(c[slot], n)
            clear(WEST_AT[slot + 1], 48)
            clear(ROWS_AT[slot + 1], 160)
        pl.when(jnp.logical_not(frames[slot][0]))(absent)
    for d in (2, 3):
        def edge_clear(d=d):
            for slot in range(3):
                present = None if slot == 0 else frames[slot - 1][0]
                start, n = piece(slot, d)
                when(present, lambda start=start, n=n: clear(start, n))
        pl.when(jnp.logical_not(dirs[d][0]))(edge_clear)

    j = lax.broadcasted_iota(jnp.int32, (1, KEYS), 1)
    extra = jnp.zeros((1, KEYS), F32)

    def bar(extra, cond, start, n):
        off = (j >= start) & (j < start + n) & jnp.logical_not(cond)
        return jnp.where(off, MASKED, extra)

    for slot in range(2):
        for n, c in zip(CHUNK_ROWS, CHUNK_AT):
            extra = bar(extra, frames[slot][0], c[slot], n)
        extra = bar(extra, frames[slot][0], WEST_AT[slot + 1], 48)
        extra = bar(extra, frames[slot][0], ROWS_AT[slot + 1], 160)
    for slot in range(3):
        for d in (2, 3):
            extra = bar(extra, dirs[d][0], *piece(slot, d))

    def rms(p, gain):
        ms = jnp.mean(p * p, axis=-1, keepdims=True)
        return (p * lax.rsqrt(ms + 1e-06) * gain).astype(BF)

    def keys_of(start, n):
        p = jnp.dot(xs[start : start + n, :], wk[...], preferred_element_type=F32)
        ks[start : start + n, :] = rms(p, row(kgain_ref))

    def values_of(start, n):
        vs[start : start + n, :] = jnp.dot(
            xs[start : start + n, :], wv[...], preferred_element_type=F32
        ).astype(BF)

    def attend(start, n, first, last):
        @pl.loop(0, HEADS // GROUP)
        def _(g):
            heads = [g * GROUP + u for u in range(GROUP)]
            at = [pl.ds(pl.multiple_of(h * HEAD_DIM, HEAD_DIM), HEAD_DIM) for h in heads]
            for u in range(GROUP):
                score[u, :, 0:n] = lax.dot_general(
                    qs[:, at[u]], ks[start : start + n, at[u]], (((1,), (1,)), ((), ())), preferred_element_type=F32
                )
            for u in range(GROUP):
                for r in range(0, TOKENS, 16):
                    rs = slice(r, r + 16)
                    s = score[u, rs, 0:n] * SCALE + bias[rs, start : start + n].astype(F32)
                    m = jnp.max(s, axis=-1, keepdims=True)
                    p = jnp.exp2(s - m)
                    new_m[u, rs] = jnp.broadcast_to(m, (16, HEAD_DIM))
                    new_l[u, rs] = jnp.broadcast_to(jnp.sum(p, axis=-1, keepdims=True), (16, HEAD_DIM))
                    prob[u, rs, 0:n] = p.astype(BF)
                pv = jnp.dot(prob[u, :, 0:n], vs[start : start + n, at[u]], preferred_element_type=F32)
                if first:
                    acc[:, at[u]] = pv
                    m_ref[heads[u]] = new_m[u]
                    l_ref[heads[u]] = new_l[u]
                else:
                    m1, m2 = m_ref[heads[u]], new_m[u]
                    m = jnp.maximum(m1, m2)
                    a1, a2 = jnp.exp2(m1 - m), jnp.exp2(m2 - m)
                    total = a1 * l_ref[heads[u]] + a2 * new_l[u]
                    joined = a1 * acc[:, at[u]] + a2 * pv
                    if last:
                        qs[:, at[u]] = (joined / total).astype(BF)
                    else:
                        acc[:, at[u]] = joined
                        m_ref[heads[u]] = m
                        l_ref[heads[u]] = total

    def each(fn, slots=(0, 1)):
        for slot in slots:
            pl.when(frames[slot][0])(functools.partial(fn, slot))

    loads[0].wait()
    qs[...] = rms(jnp.dot(xs[0:TOKENS, :], wq[...], preferred_element_type=F32), row(qgain_ref))
    loads[1].wait()
    keys_of(0, 256)
    loads[2].wait()
    bias[...] = jnp.minimum(bias_in[...].astype(F32), extra).astype(BF)
    loads[3].wait()
    values_of(0, 256)

    y_sent(0)
    y_start(1)

    def columns_on(slot):
        y_arrived(0, slot).wait_recv()
        h_start(slot + 1, (1,))

    each(columns_on)
    h_wait(0, (0, 1))
    y_start(2)
    pack(0)
    h_start(0, (2, 3))
    keys_of(256, 96)
    values_of(256, 96)
    keys_of(512, 96)
    values_of(512, 96)
    h_wait(0, (2, 3))
    keys_of(352, 160)
    values_of(352, 160)
    y_start(3)
    attend(0, 512, True, False)

    def rows_on(slot):
        y_arrived(1, slot).wait_recv()
        y_arrived(2, slot).wait_recv()
        h_wait(slot + 1, (0,))
        pack(slot + 1)
        h_start(slot + 1, (2, 3))

    each(rows_on)
    keys_of(608, 416)
    values_of(608, 416)
    attend(512, 512, False, False)
    each(lambda slot: y_arrived(3, slot).wait_recv())
    each(lambda slot: h_wait(slot + 1, (2, 3)))
    keys_of(1024, 512)
    values_of(1024, 512)
    attend(1024, 512, False, True)

    loads[4].wait()
    out_ref[...] = (jnp.dot(qs[...], wo[...], preferred_element_type=F32) * row(gate_ref)).astype(BF)

    for chunk in (1, 2, 3):
        y_sent(chunk)
    h_sent(0, range(4))
    each(lambda slot: h_sent(slot + 1, (1, 2, 3)))


def shards(latents, ada_shift, ada_scale, ada_gate, w_query, w_key, w_value, w_out, query_gain, key_gain):
    select, pack, bias = tables()
    vmem = pl.BlockSpec(memory_space=pltpu.VMEM)
    hbm = pl.BlockSpec(memory_space=pl.ANY)
    out = pl.pallas_call(
        kernel,
        out_shape=jax.ShapeDtypeStruct((TOKENS, D), BF),
        in_specs=[vmem] * 6 + [hbm] * 4 + [vmem] * 2 + [hbm],
        out_specs=vmem,
        scratch_shapes=[pltpu.VMEM((D, D), BF)] * 4
        + [
            pltpu.VMEM((KEYS, D), BF),
            pltpu.VMEM((KEYS, D), BF),
            pltpu.VMEM((KEYS, D), BF),
            pltpu.VMEM((TOKENS, D), BF),
            pltpu.VMEM((TOKENS, D), BF),
            pltpu.VMEM((3, 160, D), BF),
            pltpu.VMEM((TOKENS, KEYS), BF),
            pltpu.VMEM((TOKENS, KEYS), BF),
            pltpu.VMEM((TOKENS, D), F32),
            pltpu.VMEM((HEADS, TOKENS, HEAD_DIM), F32),
            pltpu.VMEM((HEADS, TOKENS, HEAD_DIM), F32),
            pltpu.VMEM((GROUP, TOKENS, 512), F32),
            pltpu.VMEM((GROUP, TOKENS, 512), BF),
            pltpu.VMEM((GROUP, TOKENS, HEAD_DIM), F32),
            pltpu.VMEM((GROUP, TOKENS, HEAD_DIM), F32),
            pltpu.SemaphoreType.DMA((5,)),
            pltpu.SemaphoreType.DMA((4, 2)),
            pltpu.SemaphoreType.DMA((4, 2)),
            pltpu.SemaphoreType.DMA((3, 4)),
            pltpu.SemaphoreType.DMA((3, 4)),
        ],
        compiler_params=pltpu.CompilerParams(
            collective_id=0, has_side_effects=True, vmem_limit_bytes=62 * 2**20
        ),
        cost_estimate=pl.CostEstimate(flops=2 * 10**10, bytes_accessed=2 * 10**7, transcendentals=5 * 10**6),
    )(
        latents.reshape(TOKENS, D), ada_shift, ada_scale, ada_gate, query_gain, key_gain,
        w_query, w_key, w_value, w_out,
        jnp.asarray(select, BF), jnp.asarray(pack, BF), jnp.asarray(bias, BF),
    )
    return out.reshape(latents.shape)


def solution(mesh):
    return jax.shard_map(
        shards,
        mesh=mesh,
        in_specs=(P("tm", "lat", "lon", None),) + (P(),) * 9,
        out_specs=P("tm", "lat", "lon", None),
        check_vma=False,
    )
```

time: 75 us -> 50.8 us (0.68)
  the two profiles are of different devices: /device:TPU:16 before, /device:TPU:17 now
where the time goes in v2:
time: 50.8 us; the launch traced here: 50.7 us
  Pallas kernels  48.6 us (96%)
  local copies, waits for them, and re-layouts  2.06 us (4%)
    pallas_call x1, Pallas kernels, shards(): pl.pallas_call(kernel, out_shape=jax.ShapeDtypeStruct((TOKENS, D), BF), i...  48.6 us
    unnamed x1, local copies, waits for them, and re-layouts  2.06 us

profile of v2, /device:TPU:17, one launch (start us, length us, event | category | flops | bytes accessed | tf_op | source)
XLA Modules:
  0.0 50.7 jit_solution(11418425758972459029)
XLA Ops:
  0.0 48.6 %shard_map.127 = bf16[256,1536]{1,0:T(8,128)(2,1)} custom-call(bf16[256,1536]{1,0:T(8,128)(2,1)} %bitcast.3, f32[1536]{0:T(1024)} %shift_ref.1, f32[1536]{0:T(1024)} %scale_ref.1, f32[1536]{0:T(1024)} %gate_ref.1, f32[1536]{0:T(1024)} %qgain_ref.1, f32[1536]{0:T(1024)} %kgain_ref.1, bf16[1536,1536]{1,0:T(8,128)(2,1)} %wq_any.1, bf16[1536,1536]{1,0:T(8,128)(2,1)} %wk_any.1, ...), custom_call_target="tpu_custom_call" | custom-call | flops 20000000000 | bytes 20000000 | tf_op jit(solution)/shard_map/pallas_call | solution.py:359
  48.6 2.1 %copy.15 = bf16[1,16,16,1536]{3,2,1,0:T(8,128)(2,1)} copy(bf16[1,16,16,1536]{3,2,1,0:T(8,128)(2,1)} %bitcast.2) | data formatting | bytes 1572864

commit v3 on v2

--- a/solution.py
+++ b/solution.py
@@ -24,10 +24,10 @@
 
 CHUNKS = ((0, 48), (48, 112), None, (160, 96))
 CHUNK_ROWS = (48, 112, 48, 96)
-CHUNK_AT = ((512, 560), (608, 720), (832, 880), (1024, 1120))
+CHUNK_AT = ((352, 400), (448, 560), (672, 720), (1024, 1120))
 HALO_E = 304
-WEST_AT = (256, 928, 976)
-ROWS_AT = (352, 1216, 1376)
+WEST_AT = (256, 768, 816)
+ROWS_AT = (864, 1216, 1376)
 
 
 def center_order():
@@ -79,9 +79,9 @@
 
 def kernel(
     x_ref, shift_ref, scale_ref, gate_ref, qgain_ref, kgain_ref, wq_any, wk_any, wv_any, wo_any,
-    select_ref, pack_ref, bias_any, out_ref,
+    select_ref, pack_ref, bias_any, out_any,
     wq, wk, wv, wo, xs, ks, vs, qs, staged, packed, bias_in, bias, acc, m_ref, l_ref, score, prob, new_m, new_l,
-    w_sem, y_send, y_recv, h_send, h_recv,
+    w_sem, o_sem, y_send, y_recv, h_send, h_recv,
 ):
     t, a, o = lax.axis_index("tm"), lax.axis_index("lat"), lax.axis_index("lon")
     west, east = lax.rem(o + 7, 8), lax.rem(o + 1, 8)
@@ -299,57 +299,63 @@
     qs[...] = rms(jnp.dot(xs[0:TOKENS, :], wq[...], preferred_element_type=F32), row(qgain_ref))
     loads[1].wait()
     keys_of(0, 256)
+    y_sent(0)
+    y_start(1)
     loads[2].wait()
     bias[...] = jnp.minimum(bias_in[...].astype(F32), extra).astype(BF)
     loads[3].wait()
     values_of(0, 256)
 
-    y_sent(0)
-    y_start(1)
-
     def columns_on(slot):
         y_arrived(0, slot).wait_recv()
         h_start(slot + 1, (1,))
 
     each(columns_on)
+    attend(0, 256, True, False)
+    keys_of(352, 96)
+    values_of(352, 96)
     h_wait(0, (0, 1))
     y_start(2)
     pack(0)
     h_start(0, (2, 3))
     keys_of(256, 96)
     values_of(256, 96)
-    keys_of(512, 96)
-    values_of(512, 96)
-    h_wait(0, (2, 3))
-    keys_of(352, 160)
-    values_of(352, 160)
+    each(lambda slot: y_arrived(1, slot).wait_recv())
     y_start(3)
-    attend(0, 512, True, False)
+    keys_of(448, 224)
+    values_of(448, 224)
 
     def rows_on(slot):
-        y_arrived(1, slot).wait_recv()
         y_arrived(2, slot).wait_recv()
         h_wait(slot + 1, (0,))
         pack(slot + 1)
         h_start(slot + 1, (2, 3))
 
     each(rows_on)
-    keys_of(608, 416)
-    values_of(608, 416)
-    attend(512, 512, False, False)
+    h_wait(0, (2, 3))
+    keys_of(672, 352)
+    values_of(672, 352)
+    attend(256, 768, False, False)
     each(lambda slot: y_arrived(3, slot).wait_recv())
     each(lambda slot: h_wait(slot + 1, (2, 3)))
     keys_of(1024, 512)
     values_of(1024, 512)
     attend(1024, 512, False, True)
 
-    loads[4].wait()
-    out_ref[...] = (jnp.dot(qs[...], wo[...], preferred_element_type=F32) * row(gate_ref)).astype(BF)
-
     for chunk in (1, 2, 3):
         y_sent(chunk)
     h_sent(0, range(4))
     each(lambda slot: h_sent(slot + 1, (1, 2, 3)))
+    loads[4].wait()
+    stores = []
+    for i in range(3):
+        cols = slice(512 * i, 512 * i + 512)
+        product = jnp.dot(qs[...], wo[:, cols], preferred_element_type=F32)
+        staged[:, cols] = (product * gate_ref[cols].reshape(1, 512)).astype(BF)
+        stores.append(pltpu.make_async_copy(staged.at[:, cols], out_any.at[:, cols], o_sem.at[i]))
+        stores[-1].start()
+    for store in stores:
+        store.wait()
 
 
 def shards(latents, ada_shift, ada_scale, ada_gate, w_query, w_key, w_value, w_out, query_gain, key_gain):
@@ -360,7 +366,7 @@
         kernel,
         out_shape=jax.ShapeDtypeStruct((TOKENS, D), BF),
         in_specs=[vmem] * 6 + [hbm] * 4 + [vmem] * 2 + [hbm],
-        out_specs=vmem,
+        out_specs=hbm,
         scratch_shapes=[pltpu.VMEM((D, D), BF)] * 4
         + [
             pltpu.VMEM((KEYS, D), BF),
@@ -374,11 +380,12 @@
             pltpu.VMEM((TOKENS, D), F32),
             pltpu.VMEM((HEADS, TOKENS, HEAD_DIM), F32),
             pltpu.VMEM((HEADS, TOKENS, HEAD_DIM), F32),
-            pltpu.VMEM((GROUP, TOKENS, 512), F32),
-            pltpu.VMEM((GROUP, TOKENS, 512), BF),
+            pltpu.VMEM((GROUP, TOKENS, 768), F32),
+            pltpu.VMEM((GROUP, TOKENS, 768), BF),
             pltpu.VMEM((GROUP, TOKENS, HEAD_DIM), F32),
             pltpu.VMEM((GROUP, TOKENS, HEAD_DIM), F32),
             pltpu.SemaphoreType.DMA((5,)),
+            pltpu.SemaphoreType.DMA((3,)),
             pltpu.SemaphoreType.DMA((4, 2)),
             pltpu.SemaphoreType.DMA((4, 2)),
             pltpu.SemaphoreType.DMA((3, 4)),

time: 50.8 us -> 47 us (0.925)
  the two profiles are of different devices: /device:TPU:17 before, /device:TPU:16 now
where the time goes in v3:
time: 47 us; the launch traced here: 46.5 us
  Pallas kernels  44.5 us (95%)
  local copies, waits for them, and re-layouts  2.06 us (4%)
    pallas_call x1, Pallas kernels, shards(): pl.pallas_call(kernel, out_shape=jax.ShapeDtypeStruct((TOKENS, D), BF), i...  44.5 us
    unnamed x1, local copies, waits for them, and re-layouts  2.06 us

profile of v3, /device:TPU:16, one launch (start us, length us, event | category | flops | bytes accessed | tf_op | source)
XLA Modules:
  0.0 46.5 jit_solution(12714300379497649501)
XLA Ops:
  0.0 44.5 %shard_map.127 = bf16[256,1536]{1,0:T(8,128)(2,1)} custom-call(bf16[256,1536]{1,0:T(8,128)(2,1)} %bitcast.3, f32[1536]{0:T(1024)} %shift_ref.1, f32[1536]{0:T(1024)} %scale_ref.1, f32[1536]{0:T(1024)} %gate_ref.1, f32[1536]{0:T(1024)} %qgain_ref.1, f32[1536]{0:T(1024)} %kgain_ref.1, bf16[1536,1536]{1,0:T(8,128)(2,1)} %wq_any.1, bf16[1536,1536]{1,0:T(8,128)(2,1)} %wk_any.1, ...), custom_call_target="tpu_custom_call" | custom-call | flops 20000000000 | bytes 20000000 | tf_op jit(solution)/shard_map/pallas_call | solution.py:365
  44.5 2.1 %copy.15 = bf16[1,16,16,1536]{3,2,1,0:T(8,128)(2,1)} copy(bf16[1,16,16,1536]{3,2,1,0:T(8,128)(2,1)} %bitcast.2) | data formatting | bytes 1572864

commit v4 on v3

--- a/solution.py
+++ b/solution.py
@@ -19,7 +19,7 @@
 F32 = jnp.float32
 MESH = pl.DeviceIdType.MESH
 MASKED = -1e30
-GROUP = 4
+GROUP = 6
 SCALE = HEAD_DIM ** (-0.5) * math.log2(math.e)
 
 CHUNKS = ((0, 48), (48, 112), None, (160, 96))
@@ -78,9 +78,9 @@
 
 
 def kernel(
-    x_ref, shift_ref, scale_ref, gate_ref, qgain_ref, kgain_ref, wq_any, wk_any, wv_any, wo_any,
-    select_ref, pack_ref, bias_any, out_any,
-    wq, wk, wv, wo, xs, ks, vs, qs, staged, packed, bias_in, bias, acc, m_ref, l_ref, score, prob, new_m, new_l,
+    x_any, shift_any, scale_any, qgain_any, kgain_any, wq_any, wk_any, wv_any, select_any, pack_any, bias_any,
+    wo_any, gate_any, out_any,
+    x_ref, shift_ref, scale_ref, qgain_ref, kgain_ref, wq, wk, wv, select_ref, pack_ref, wo, gate_ref, xs, ks, vs, qs, staged, packed, bias_in, bias, acc, m_ref, l_ref, score, prob, new_m, new_l,
     w_sem, o_sem, y_send, y_recv, h_send, h_recv,
 ):
     t, a, o = lax.axis_index("tm"), lax.axis_index("lat"), lax.axis_index("lon")
@@ -100,29 +100,36 @@
         else:
             pl.when(cond)(fn)
 
-    loads = []
-    pairs = ((wq_any, wq), (wk_any, wk), (bias_any, bias_in), (wv_any, wv), (wo_any, wo))
-    for i, (src, dst) in enumerate(pairs):
-        loads.append(pltpu.make_async_copy(src, dst, w_sem.at[i]))
-        loads[-1].start()
-
     barrier = pltpu.get_barrier_semaphore()
     for cond, dev in dirs + frames:
         when(cond, lambda dev=dev: pl.semaphore_signal(barrier, inc=1, device_id=dev, device_id_type=MESH))
 
+    pairs = (
+        (x_any, x_ref), (shift_any, shift_ref), (scale_any, scale_ref), (select_any, select_ref),
+        (wq_any, wq), (qgain_any, qgain_ref), (wk_any, wk), (kgain_any, kgain_ref),
+        (bias_any, bias_in), (wv_any, wv), (pack_any, pack_ref), (wo_any, wo), (gate_any, gate_ref),
+    )
+    loads = [pltpu.make_async_copy(src, dst, w_sem.at[i]) for i, (src, dst) in enumerate(pairs)]
+    for load in loads[:3]:
+        load.start()
+
     one = lambda c: jnp.where(c, 1, 0)
 
     row = lambda ref: ref[...].reshape(1, D)
+    for load in loads[:3]:
+        load.wait()
+    for load in loads[3:]:
+        load.start()
     shift, scale = row(shift_ref), 1.0 + row(scale_ref)
 
-    @pl.loop(0, 8)
-    def _(i):
-        rows = pl.ds(pl.multiple_of(i * 32, 32), 32)
+    for i in range(8):
+        rows = slice(32 * i, 32 * i + 32)
         v = x_ref[rows, :].astype(F32)
         centred = v - jnp.mean(v, axis=-1, keepdims=True)
         var = jnp.mean(centred * centred, axis=-1, keepdims=True)
         xs[rows, :] = (centred * lax.rsqrt(var + 1e-06) * scale + shift).astype(BF)
 
+    loads[3].wait()
     staged[...] = jnp.dot(select_ref[...], xs[0:TOKENS, :], preferred_element_type=F32).astype(BF)
     pl.semaphore_wait(barrier, 2 + one(has_prev) + one(has_next) + one(has_north) + one(has_south))
 
@@ -295,15 +302,18 @@
         for slot in slots:
             pl.when(frames[slot][0])(functools.partial(fn, slot))
 
-    loads[0].wait()
+    loads[4].wait()
+    loads[5].wait()
     qs[...] = rms(jnp.dot(xs[0:TOKENS, :], wq[...], preferred_element_type=F32), row(qgain_ref))
-    loads[1].wait()
+    loads[6].wait()
+    loads[7].wait()
     keys_of(0, 256)
     y_sent(0)
     y_start(1)
-    loads[2].wait()
+    loads[8].wait()
     bias[...] = jnp.minimum(bias_in[...].astype(F32), extra).astype(BF)
-    loads[3].wait()
+    loads[9].wait()
+    loads[10].wait()
     values_of(0, 256)
 
     def columns_on(slot):
@@ -321,7 +331,6 @@
     keys_of(256, 96)
     values_of(256, 96)
     each(lambda slot: y_arrived(1, slot).wait_recv())
-    y_start(3)
     keys_of(448, 224)
     values_of(448, 224)
 
@@ -332,6 +341,7 @@
         h_start(slot + 1, (2, 3))
 
     each(rows_on)
+    y_start(3)
     h_wait(0, (2, 3))
     keys_of(672, 352)
     values_of(672, 352)
@@ -346,7 +356,8 @@
         y_sent(chunk)
     h_sent(0, range(4))
     each(lambda slot: h_sent(slot + 1, (1, 2, 3)))
-    loads[4].wait()
+    for load in loads[11:]:
+        load.wait()
     stores = []
     for i in range(3):
         cols = slice(512 * i, 512 * i + 512)
@@ -360,15 +371,22 @@
 
 def shards(latents, ada_shift, ada_scale, ada_gate, w_query, w_key, w_value, w_out, query_gain, key_gain):
     select, pack, bias = tables()
-    vmem = pl.BlockSpec(memory_space=pltpu.VMEM)
     hbm = pl.BlockSpec(memory_space=pl.ANY)
+    vector = pltpu.VMEM((D,), F32)
+    square = pltpu.VMEM((D, D), BF)
     out = pl.pallas_call(
         kernel,
         out_shape=jax.ShapeDtypeStruct((TOKENS, D), BF),
-        in_specs=[vmem] * 6 + [hbm] * 4 + [vmem] * 2 + [hbm],
+        in_specs=[hbm] * 13,
         out_specs=hbm,
-        scratch_shapes=[pltpu.VMEM((D, D), BF)] * 4
+        scratch_shapes=[pltpu.VMEM((TOKENS, D), BF)]
+        + [vector] * 4
+        + [square] * 3
         + [
+            pltpu.VMEM((TOKENS, TOKENS), BF),
+            pltpu.VMEM((160, TOKENS), BF),
+            square,
+            vector,
             pltpu.VMEM((KEYS, D), BF),
             pltpu.VMEM((KEYS, D), BF),
             pltpu.VMEM((KEYS, D), BF),
@@ -384,7 +402,7 @@
             pltpu.VMEM((GROUP, TOKENS, 768), BF),
             pltpu.VMEM((GROUP, TOKENS, HEAD_DIM), F32),
             pltpu.VMEM((GROUP, TOKENS, HEAD_DIM), F32),
-            pltpu.SemaphoreType.DMA((5,)),
+            pltpu.SemaphoreType.DMA((13,)),
             pltpu.SemaphoreType.DMA((3,)),
             pltpu.SemaphoreType.DMA((4, 2)),
             pltpu.SemaphoreType.DMA((4, 2)),
@@ -396,9 +414,9 @@
         ),
         cost_estimate=pl.CostEstimate(flops=2 * 10**10, bytes_accessed=2 * 10**7, transcendentals=5 * 10**6),
     )(
-        latents.reshape(TOKENS, D), ada_shift, ada_scale, ada_gate, query_gain, key_gain,
-        w_query, w_key, w_value, w_out,
+        latents.reshape(TOKENS, D), ada_shift, ada_scale, query_gain, key_gain, w_query, w_key, w_value,
         jnp.asarray(select, BF), jnp.asarray(pack, BF), jnp.asarray(bias, BF),
+        w_out, ada_gate,
     )
     return out.reshape(latents.shape)
 

time: 47 us -> 44.9 us (0.955)
  Pallas kernels: 44.5 us -> 42.6 us
    pallas_call x1, Pallas kernels: 44.5 us -> 42.6 us  [shards(): pl.pallas_call(kernel, out_shape=jax.ShapeDtypeStruct((TOKENS, D), BF), i...]
where the time goes in v4:
time: 44.9 us; the launch traced here: 44.6 us
  Pallas kernels  42.6 us (95%)
  local copies, waits for them, and re-layouts  2.06 us (5%)
    pallas_call x1, Pallas kernels, shards(): pl.pallas_call(kernel, out_shape=jax.ShapeDtypeStruct((TOKENS, D), BF), i...  42.6 us
    unnamed x1, local copies, waits for them, and re-layouts  2.06 us

profile of v4, /device:TPU:16, one launch (start us, length us, event | category | flops | bytes accessed | tf_op | source)
XLA Modules:
  0.0 44.6 jit_solution(14310132409574682273)
XLA Ops:
  0.0 42.6 %shard_map.127 = bf16[256,1536]{1,0:T(8,128)(2,1)} custom-call(bf16[256,1536]{1,0:T(8,128)(2,1)} %bitcast.3, f32[1536]{0:T(1024)} %shift_any.1, f32[1536]{0:T(1024)} %scale_any.1, f32[1536]{0:T(1024)} %qgain_any.1, f32[1536]{0:T(1024)} %kgain_any.1, bf16[1536,1536]{1,0:T(8,128)(2,1)} %wq_any.1, bf16[1536,1536]{1,0:T(8,128)(2,1)} %wk_any.1, ...), custom_call_target="tpu_custom_call" | custom-call | flops 20000000000 | bytes 20000000 | tf_op jit(solution)/shard_map/pallas_call | solution.py:377
  42.6 2.1 %copy.15 = bf16[1,16,16,1536]{3,2,1,0:T(8,128)(2,1)} copy(bf16[1,16,16,1536]{3,2,1,0:T(8,128)(2,1)} %bitcast.2) | data formatting | bytes 1572864

commit v5 on v4

--- a/solution.py
+++ b/solution.py
@@ -263,10 +263,9 @@
         ).astype(BF)
 
     def attend(start, n, first, last):
-        @pl.loop(0, HEADS // GROUP)
-        def _(g):
+        for g in range(HEADS // GROUP):
             heads = [g * GROUP + u for u in range(GROUP)]
-            at = [pl.ds(pl.multiple_of(h * HEAD_DIM, HEAD_DIM), HEAD_DIM) for h in heads]
+            at = [pl.ds(h * HEAD_DIM, HEAD_DIM) for h in heads]
             for u in range(GROUP):
                 score[u, :, 0:n] = lax.dot_general(
                     qs[:, at[u]], ks[start : start + n, at[u]], (((1,), (1,)), ((), ())), preferred_element_type=F32

time: 44.9 us -> 44 us (0.980)
  Pallas kernels: 42.6 us -> 41.5 us
    pallas_call x1, Pallas kernels: 42.6 us -> 41.5 us  [shards(): pl.pallas_call(kernel, out_shape=jax.ShapeDtypeStruct((TOKENS, D), BF), i...]
where the time goes in v5:
time: 44 us; the launch traced here: 43.6 us
  Pallas kernels  41.5 us (94%)
  local copies, waits for them, and re-layouts  2.06 us (5%)
    pallas_call x1, Pallas kernels, shards(): pl.pallas_call(kernel, out_shape=jax.ShapeDtypeStruct((TOKENS, D), BF), i...  41.5 us
    unnamed x1, local copies, waits for them, and re-layouts  2.06 us

profile of v5, /device:TPU:16, one launch (start us, length us, event | category | flops | bytes accessed | tf_op | source)
XLA Modules:
  0.0 43.6 jit_solution(545324358011848029)
XLA Ops:
  0.0 41.5 %shard_map.127 = bf16[256,1536]{1,0:T(8,128)(2,1)} custom-call(bf16[256,1536]{1,0:T(8,128)(2,1)} %bitcast.3, f32[1536]{0:T(1024)} %shift_any.1, f32[1536]{0:T(1024)} %scale_any.1, f32[1536]{0:T(1024)} %qgain_any.1, f32[1536]{0:T(1024)} %kgain_any.1, bf16[1536,1536]{1,0:T(8,128)(2,1)} %wq_any.1, bf16[1536,1536]{1,0:T(8,128)(2,1)} %wk_any.1, ...), custom_call_target="tpu_custom_call" | custom-call | flops 20000000000 | bytes 20000000 | tf_op jit(solution)/shard_map/pallas_call | solution.py:376
  41.5 2.1 %copy.15 = bf16[1,16,16,1536]{3,2,1,0:T(8,128)(2,1)} copy(bf16[1,16,16,1536]{3,2,1,0:T(8,128)(2,1)} %bitcast.2) | data formatting | bytes 1572864
